TPU v7x, 32 devices: a whole 2x2x4 slice. The times are simulated.
32 devices in a mesh: row: 4 (over z), ma: 8 (over y, x, core).
Axes of the slice: x: 2, y: 2, z: 4, core: 2. Of those that a mesh axis runs over, the one named last changes fastest.
Arguments:
- spectra: float32 [4, 2, 128, 4224], P(None, None, 'row', 'ma'), may hold values from -6 to 6
- dtheta_table: bfloat16 [4224, 768], P('ma'), may hold values from -0.046875 to 0.046875
- dphi_table: bfloat16 [4224, 768], P('ma'), may hold values from -0.046875 to 0.046875
- analysis_table: bfloat16 [4224, 768], P('ma'), may hold values from -6 to 6
- pair_index: int32 [8], replicated, may hold values from 0 to 255, as said below
- diffusivity: float32 [4], replicated, may hold values from 0.0001 to 0.0004
Outputs:
- new_spectra: float32 [4, 2, 128, 4224], P(None, None, 'row', 'ma')
Inputs may be any that keep to these rules, and one draw needn't show every extreme that they name: 8 distinct values, among them always both 0 and the largest; position g holds the orders pair_index[g] and 511 - pair_index[g].
All inputs are finite; a program needn't handle non-finite values.
Results may differ from a plain program's by a relative error of at most 0.0057.
Values may be sent and summed in bfloat16 or wider, within the bound.
A program may use at most 64 MiB of HBM per device.

v0:
```python
import math
import jax
import jax.numpy as jnp
from jax import lax
from jax.sharding import PartitionSpec as P

LMAX = 511
NPHI = 1536
SLOTS = 528
ROTATION = 2.0
SHELL_RADIUS = 16.0


def slot_layout(pair_values):
    slot_index = jnp.arange(SLOTS, dtype=jnp.int32)[None, :]
    lowest = pair_values[:, None]
    first_part = slot_index < LMAX + 1 - lowest
    second_part = jnp.logical_and(jnp.logical_not(first_part), slot_index < LMAX + 2)
    degree = jnp.where(first_part, lowest + slot_index, slot_index - 1)
    wave_order = jnp.where(first_part, lowest, LMAX - lowest)
    return (first_part, second_part, degree, wave_order)


def fourier_tables(pair_values):
    orders = jnp.stack([pair_values, LMAX - pair_values], axis=1)
    angle_step = jnp.arange(NPHI, dtype=jnp.int32)
    phases = orders[:, :, None] * angle_step[None, None, :] % NPHI
    angles = phases.astype(jnp.float32) * (2.0 * math.pi / NPHI)
    weight_order = jnp.where(orders == 0, 1.0, 2.0).astype(jnp.float32)[:, :, None]
    cosine = jnp.cos(angles)
    sine_part = jnp.sin(angles)
    synthesis = jnp.stack([weight_order * cosine, -weight_order * sine_part]).astype(jnp.bfloat16)
    analysis_fourier = (jnp.stack([cosine, -sine_part]) / NPHI).astype(jnp.bfloat16)
    return (synthesis, analysis_fourier)


def grid_products(grid_values):
    stream_theta, stream_phi, poloidal_theta, poloidal_phi = (
        grid_values[0],
        grid_values[1],
        grid_values[2],
        grid_values[3],
    )
    thermal_theta, thermal_phi, magnetic_theta, magnetic_phi = (
        grid_values[4],
        grid_values[5],
        grid_values[6],
        grid_values[7],
    )
    flow_theta = poloidal_theta - stream_phi
    flow_phi = poloidal_phi + stream_theta
    field_theta = -magnetic_phi
    stress = field_theta * magnetic_theta - flow_theta * flow_phi
    pressure = 0.5 * (magnetic_theta * magnetic_theta - field_theta * field_theta) - 0.5 * (
        flow_phi * flow_phi - flow_theta * flow_theta
    )
    heat_flux = -(flow_theta * thermal_theta + flow_phi * thermal_phi)
    induction = -(flow_theta * magnetic_theta - flow_phi * field_theta)
    return jnp.stack([stress, pressure, heat_flux, induction])


def coupled(source, partner, parity, degree, wave_order, alive):
    degree_real = degree.astype(jnp.float32)
    order_real = wave_order.astype(jnp.float32)
    lower_coupling = jnp.sqrt(
        (degree_real * degree_real - order_real * order_real)
        * alive
        / jnp.maximum(4.0 * degree_real * degree_real - 1.0, 1.0)
    )
    upper_degree = degree_real + 1.0
    upper_coupling = (
        jnp.sqrt(
            (upper_degree * upper_degree - order_real * order_real)
            / (4.0 * upper_degree * upper_degree - 1.0)
        )
        * alive
        * (degree < LMAX).astype(jnp.float32)
    )
    spin_term = order_real / (degree_real * (degree_real + 1.0) + 2.0)
    turned = jnp.stack([-source[1], source[0]])
    below_slot = jnp.concatenate([jnp.zeros_like(partner[..., :1]), partner[..., :-1]], axis=-1)
    above_slot = jnp.concatenate([partner[..., 1:], jnp.zeros_like(partner[..., :1])], axis=-1)
    return ROTATION * (
        spin_term * turned + parity * (lower_coupling * below_slot + upper_coupling * above_slot)
    )


def radial_solve(right_side, degree_flat, diffusivity):
    points = right_side.shape[2]
    counter = jnp.arange(1, points + 1, dtype=jnp.int32)
    product = counter[:, None] * counter[None, :] % (2 * (points + 1))
    sine_basis = math.sqrt(2.0 / (points + 1)) * jnp.sin(
        product.astype(jnp.float32) * (math.pi / (points + 1))
    )
    eigenvalues = (
        4.0
        * (points + 1)
        * (points + 1)
        * jnp.sin(counter.astype(jnp.float32) * (math.pi / (2 * (points + 1)))) ** 2
    )
    degree_real = degree_flat.astype(jnp.float32)
    horizontal = degree_real * (degree_real + 1.0) / (SHELL_RADIUS * SHELL_RADIUS)
    modal_part = jnp.einsum(
        "jk,fcks->fcjs", sine_basis, right_side, precision=lax.Precision.HIGHEST
    )
    factor = 1.0 + diffusivity[:, None, None, None] * (
        eigenvalues[None, None, :, None] + horizontal[None, None, None, :]
    )
    return jnp.einsum(
        "jk,fcks->fcjs", sine_basis, modal_part / factor, precision=lax.Precision.HIGHEST
    )


def local(spectra, dtheta_table, dphi_table, analysis_table, pair_index, diffusivity):
    local_pairs = spectra.shape[3] // SLOTS
    radius_count = spectra.shape[2]
    theta_count = dtheta_table.shape[1]
    columns = local_pairs * SLOTS
    own_pairs = lax.dynamic_slice_in_dim(
        pair_index, lax.axis_index("ma") * local_pairs, local_pairs
    )
    first_part, second_part, degree, wave_order = slot_layout(own_pairs)
    alive = jnp.logical_or(first_part, second_part).astype(jnp.float32)
    part_masks = jnp.stack([first_part, second_part], axis=1).astype(jnp.float32)
    masked_state = spectra.reshape(4, 2, radius_count, local_pairs, SLOTS) * alive
    coeffs = masked_state.astype(jnp.bfloat16)
    spread = coeffs[:, :, :, :, None, :] * part_masks.astype(jnp.bfloat16)[None, None, None]
    theta_rows = dtheta_table.reshape(local_pairs, SLOTS, theta_count)
    phi_rows = dphi_table.reshape(local_pairs, SLOTS, theta_count)
    along_theta = jnp.einsum(
        "fcrpjs,pst->fcrpjt", spread, theta_rows, preferred_element_type=jnp.float32
    )
    phi_direct = jnp.einsum(
        "fcrpjs,pst->fcrpjt", spread, phi_rows, preferred_element_type=jnp.float32
    )
    along_phi = jnp.stack([-phi_direct[:, 1], phi_direct[:, 0]], axis=1)
    grid_spectra = jnp.stack([along_theta, along_phi], axis=1)
    grid_spectra = (
        jnp.transpose(grid_spectra, (3, 0, 1, 2, 4, 5, 6))
        .reshape(radius_count, 8, 2, local_pairs, 2, theta_count)
        .astype(jnp.bfloat16)
    )
    synthesis, analysis_fourier = fourier_tables(pair_index)

    def one_radius(radius_block):
        grid_values = jnp.einsum(
            "qcpjt,cpjk->qtk", radius_block, synthesis, preferred_element_type=jnp.float32
        )
        products = grid_products(grid_values).astype(jnp.bfloat16)
        return jnp.einsum(
            "ftk,cpjk->fcpjt", products, analysis_fourier, preferred_element_type=jnp.float32
        ).astype(jnp.bfloat16)

    latitudes = lax.all_to_all(grid_spectra, "ma", split_axis=5, concat_axis=3, tiled=True)
    computed = lax.map(one_radius, latitudes)
    returned = lax.all_to_all(computed, "ma", split_axis=3, concat_axis=5, tiled=True)
    analysis_rows = analysis_table.reshape(local_pairs, SLOTS, theta_count)
    projected = jnp.einsum(
        "rfcpjt,pst->fcrpjs", returned, analysis_rows, preferred_element_type=jnp.float32
    )
    nonlinear = jnp.sum(projected * part_masks[None, None, None], axis=4)
    forcing = jnp.stack(
        [
            coupled(masked_state[0], masked_state[1], 1.0, degree, wave_order, alive),
            coupled(masked_state[1], masked_state[0], -1.0, degree, wave_order, alive),
        ]
    )
    forcing = jnp.concatenate([forcing, jnp.zeros_like(forcing)], axis=0)
    right_side = (masked_state + nonlinear + forcing) * alive
    pencils = lax.all_to_all(
        right_side.reshape(4, 2, radius_count, columns),
        "row",
        split_axis=3,
        concat_axis=2,
        tiled=True,
    )
    share_size = columns // lax.axis_size("row")
    degree_share = lax.dynamic_slice_in_dim(
        degree.reshape(columns), lax.axis_index("row") * share_size, share_size
    )
    solved = radial_solve(pencils, degree_share, diffusivity)
    shells = lax.all_to_all(solved, "row", split_axis=2, concat_axis=3, tiled=True)
    return shells * alive.reshape(columns)


def solution(mesh):
    return jax.shard_map(
        local,
        mesh=mesh,
        in_specs=(
            P(None, None, "row", "ma"),
            P("ma", None),
            P("ma", None),
            P("ma", None),
            P(),
            P(),
        ),
        out_specs=P(None, None, "row", "ma"),
        check_vma=False,
    )
```

profile of v0, /device:TPU:2, one launch (start us, length us, event | category | flops | bytes accessed | tf_op | source)
XLA Modules:
  0.0 247.0 jit_solution(5899633462003070407)
XLA Ops:
  0.0 1.4 dynamic_slice.10
  3.3 1.2 fusion.98
  5.4 1.0 copy-done.16
  7.6 11.3 %copy.34 = bf16[32,8,2,1,2,768]{0,4,2,1,3,5:T(2,128)(2,1)} copy(bf16[32,8,2,1,2,768]{5,0,4,2,1,3:T(8,128)(2,1)S(1)} %bitcast.167) | data formatting | bytes 3145728 | tf_op jit(solution)/shard_map/convert_element_type | solution.py:141
  18.9 9.5 %reshape.518 = bf16[8,2,49152]{2,1,0:T(2,128)(2,1)} reshape(bf16[768,1,8,2,2,32]{5,4,3,2,1,0:T(2,128)(2,1)} %bitcast.163) | data formatting | bytes 3145728
  28.4 4.4 %all-to-all-start = ((bf16[8,2,49152]{2,1,0:T(2,128)(2,1)}), bf16[8,2,49152]{2,1,0:T(2,128)(2,1)S(1)}, u32[]{:S(2)}, u32[]{:S(2)}) async-start(bf16[8,2,49152]{2,1,0:T(2,128)(2,1)} %reshape.518), calls=%async_computation | async-start | bytes 3145728 | tf_op jit(solution)/shard_map/all_to_all | solution.py:154
  33.5 1.3 fusion.68
  34.8 1.3 fusion.77
  40.0 12.3 %all-to-all-done = bf16[8,2,49152]{2,1,0:T(2,128)(2,1)S(1)} async-done(((bf16[8,2,49152]{2,1,0:T(2,128)(2,1)}), bf16[8,2,49152]{2,1,0:T(2,128)(2,1)S(1)}, u32[]{:S(2)}, u32[]{:S(2)}) %all-to-all-start) | async-done | bytes 1572896 | tf_op jit(solution)/shard_map/all_to_all | solution.py:154
  52.3 5.4 %reshape.519 = bf16[768,1,8,2,2,32]{5,4,3,2,1,0:T(2,128)(2,1)} reshape(bf16[8,2,49152]{2,1,0:T(2,128)(2,1)S(1)} %all-to-all-done) | data formatting | bytes 3145728
  57.7 11.0 %copy.35 = bf16[32,8,2,1,2,8,96]{6,5,4,1,2,0,3:T(8,128)(2,1)S(1)} copy(bf16[32,8,2,1,2,8,96]{0,4,2,1,6,5,3:T(2,128)(2,1)} %bitcast.164) | data formatting | bytes 3145728 | tf_op jit(solution)/shard_map/all_to_all | solution.py:154
  68.7 86.1 %while.10 = (s32[]{:T(128)}, bf16[32,4,2,8,2,96]{5,4,2,1,0,3:T(2,128)(2,1)}, bf16[32,8,2,8,2,96]{5,3,4,1,2,0:T(8,128)(2,1)S(1)}, bf16[2,8,2,1536]{3,1,2,0:T(8,12...) while((s32[]{:T(128)}, bf16[32,4,2,8,2,96]{5,4,2,1,0,3:T(2,128)(2,1)}, ...), condition=%wide.region_1.2_spmd, body=%wide.region_0.1_spmd.sunk | while | flops 122105856 | bytes 15680073 | solution.py:155
  68.7 0.8 convolution_bitcast_fusion.6
  93.0 0.8 convolution_bitcast_fusion.6
  119.9 0.8 convolution_bitcast_fusion.6
  154.8 5.1 %all-to-all-start.1 = ((bf16[32,4,2,8,2,96]{5,4,2,1,0,3:T(2,128)(2,1)}), bf16[32,4,2,8,2,96]{5,4,2,1,0,3:T(2,128)(2,1)S(1)}, u32[]{:S(2)}, u32[]{:S(2)}) async-start(bf16[32,4,2,8,2,96]{5,4,2,1,0,3:T(2,128)(2,1)} %get-tuple-element.32), calls=%async_computation.1 | async-start | bytes 2097152 | tf_op jit(solution)/shard_map/all_to_all | solution.py:156
  160.4 13.5 %all-to-all-done.1 = bf16[32,4,2,8,2,96]{5,4,2,1,0,3:T(2,128)(2,1)S(1)} async-done(((bf16[32,4,2,8,2,96]{5,4,2,1,0,3:T(2,128)(2,1)}), bf16[32,4,2,8,2,96]{5,4,2,1,0,3:T(2,128)(2,1)S(1)}, u32[]{:S(2)}, u32[]{:S(2)}) %all-to-all-start.1) | async-done | bytes 786464 | tf_op jit(solution)/shard_map/all_to_all | solution.py:156
  174.6 0.9 reshape.509
  175.5 2.1 fusion.13
  177.6 1.0 fusion.22
  178.5 2.9 %copy.42 = f32[4,2,32,528]{2,1,0,3:T(2,128)S(1)} copy(f32[4,2,32,528]{3,2,1,0:T(8,128)} %fusion.22) | data formatting | bytes 1081344 | tf_op jit(solution)/shard_map/mul | solution.py:169
  181.5 2.9 %reshape.520 = f32[4,1,33792]{2,1,0:T(1,128)} reshape(f32[528,4,2,32]{3,2,1,0:T(2,128)S(1)} %bitcast.165) | data formatting | bytes 1081344
  184.4 4.9 %all-to-all-start.2 = ((f32[4,1,33792]{2,1,0:T(1,128)}), f32[4,1,33792]{2,1,0:T(1,128)S(1)}, u32[]{:S(2)}, u32[]{:S(2)}) async-start(f32[4,1,33792]{2,1,0:T(1,128)} %reshape.520), calls=%async_computation.2 | async-start | bytes 1081344 | tf_op jit(solution)/shard_map/all_to_all | solution.py:170
  189.3 1.4 fusion.85
  191.6 12.7 %all-to-all-done.2 = f32[4,1,33792]{2,1,0:T(1,128)S(1)} async-done(((f32[4,1,33792]{2,1,0:T(1,128)}), f32[4,1,33792]{2,1,0:T(1,128)S(1)}, u32[]{:S(2)}, u32[]{:S(2)}) %all-to-all-start.2) | async-done | bytes 540704 | tf_op jit(solution)/shard_map/all_to_all | solution.py:170
  204.9 2.2 reduce.1
  207.1 1.9 reshape.521
  209.0 3.0 %copy.43 = f32[4,2,32,4,132]{4,2,3,1,0:T(8,128)} copy(f32[4,2,32,4,132]{2,1,0,4,3:T(2,128)S(1)} %bitcast.166) | data formatting | bytes 1081344 | tf_op jit(solution)/shard_map/all_to_all | solution.py:170
  212.0 3.2 %fusion.15 = f32[4,2,128,132]{2,3,1,0:T(8,128)S(1)} fusion(f32[4,2,128,132]{3,2,1,0:T(8,128)} %bitcast.171, f32[4,128,132]{1,2,0:T(8,128)S(1)} %copy-done.6, s32[128]{0:T(128)S(1)} %iota_add_fusion.1), kind=kOutput, calls=%fused_computation.32 | convolution fusion | flops 207917056 | bytes 1352192 | tf_op jit(solution)/shard_map/jk,fcks->fcjs/dot_general | solution.py:103
  215.2 0.9 convolution_bitcast_fusion.3
  216.7 27.7 %all_to_all.69 = f32[4,2,128,132]{3,1,0,2:T(2,128)S(1)} all-to-all(f32[4,2,128,132]{3,1,0,2:T(2,128)S(1)} %copy.45), channel_id=1, replica_groups=mesh['row'=4,'ma'=8] {'row'}, dimensions={2} | all-to-all | bytes 1081344 | tf_op jit(solution)/shard_map/all_to_all | solution.py:182
  246.1 0.9 broadcast_multiply_fusion
  (225 shorter events, 94.6 us)
Async XLA Ops:
  0.0 4.5 %copy-start = (bf16[528,768]{1,0:T(8,128)(2,1)S(1)}, bf16[528,768]{1,0:T(8,128)(2,1)}, u32[]{:S(2)}) copy-start(bf16[528,768]{1,0:T(8,128)(2,1)} %param.10) | copy-start | bytes 2433028
  2.1 0.6 copy-start.10
  4.5 34.1 %copy-start.1 = (f32[4,2,32,528]{3,2,1,0:T(8,128)}, f32[4,2,32,528]{3,2,1,0:T(8,128)S(1)}, u32[]{:S(2)}) copy-start(f32[4,2,32,528]{3,2,1,0:T(8,128)S(1)} %get-tuple-element.47) | copy-start | bytes 1622020
  5.3 1.1 copy-start.16
  28.4 4.4 %copy-start.12 = (s32[8]{0:T(128)S(1)}, s32[8]{0:T(128)}, u32[]{:S(2)}) copy-start(s32[8]{0:T(128)} %param.12) | copy-start | bytes 100
  28.4 23.9 %all-to-all-start = ((bf16[8,2,49152]{2,1,0:T(2,128)(2,1)}), bf16[8,2,49152]{2,1,0:T(2,128)(2,1)S(1)}, u32[]{:S(2)}, u32[]{:S(2)}) async-start(bf16[8,2,49152]{2,1,0:T(2,128)(2,1)} %reshape.518), calls=%async_computation | async-start | bytes 3145728 | tf_op jit(solution)/shard_map/all_to_all | solution.py:154
  57.7 11.0 %copy-start.7 = (bf16[2,8,2,1536]{3,1,2,0:T(8,128)(2,1)S(1)}, bf16[2,8,2,1536]{3,1,2,0:T(8,128)(2,1)}, u32[]{:S(2)}) copy-start(bf16[2,8,2,1536]{3,1,2,0:T(8,128)(2,1)} %fusion.27) | copy-start | bytes 294916
  154.8 5.1 %copy-start.3 = (f32[1,2,32,1,528]{4,2,1,3,0:T(8,128)S(1)}, f32[1,2,32,1,528]{4,2,1,3,0:T(8,128)}, u32[]{:S(2)}) copy-start(f32[1,2,32,1,528]{4,2,1,3,0:T(8,128)} %get-tuple-element.54) | copy-start | bytes 405508
  154.8 5.3 %copy-start.4 = (f32[1,32,1,528]{3,1,0,2:T(8,128)S(1)}, f32[1,32,1,528]{3,1,0,2:T(8,128)}, u32[]{:S(2)}) copy-start(f32[1,32,1,528]{3,1,0,2:T(8,128)} %get-tuple-element.61) | copy-start | bytes 202756
  154.8 5.3 %copy-start.5 = (f32[1,32,1,528]{3,1,2,0:T(8,128)S(1)}, f32[1,32,1,528]{3,1,2,0:T(8,128)}, u32[]{:S(2)}) copy-start(f32[1,32,1,528]{3,1,2,0:T(8,128)} %get-tuple-element.76) | copy-start | bytes 202756
  154.8 5.3 %copy-start.8 = (f32[528]{0:T(1024)S(1)}, f32[528]{0:T(1024)}, u32[]{:S(2)}) copy-start(f32[528]{0:T(1024)} %get-tuple-element.75) | copy-start | bytes 6340
  154.8 5.3 %copy-start.9 = (f32[528]{0:T(1024)S(1)}, f32[528]{0:T(1024)}, u32[]{:S(2)}) copy-start(f32[528]{0:T(1024)} %fusion.77) | copy-start | bytes 6340
  154.8 19.0 %all-to-all-start.1 = ((bf16[32,4,2,8,2,96]{5,4,2,1,0,3:T(2,128)(2,1)}), bf16[32,4,2,8,2,96]{5,4,2,1,0,3:T(2,128)(2,1)S(1)}, u32[]{:S(2)}, u32[]{:S(2)}) async-start(bf16[32,4,2,8,2,96]{5,4,2,1,0,3:T(2,128)(2,1)} %get-tuple-element.32), calls=%async_computation.1 | async-start | bytes 2097152 | tf_op jit(solution)/shard_map/all_to_all | solution.py:156
  173.9 1.6 copy-start.11
  175.4 2.1 copy-start.2
  175.5 2.1 copy-start.15
  181.5 9.3 %copy-start.14 = (f32[128]{0:T(128)S(1)}, f32[128]{0:T(128)}, u32[]{:S(2)}) copy-start(f32[128]{0:T(128)} %multiply_multiply_fusion.2) | copy-start | bytes 1540
  181.5 9.4 %copy-start.13 = (f32[4]{0:T(128)S(1)}, f32[4]{0:T(128)}, u32[]{:S(2)}) copy-start(f32[4]{0:T(128)} %param.13) | copy-start | bytes 52
  184.4 20.0 %all-to-all-start.2 = ((f32[4,1,33792]{2,1,0:T(1,128)}), f32[4,1,33792]{2,1,0:T(1,128)S(1)}, u32[]{:S(2)}, u32[]{:S(2)}) async-start(f32[4,1,33792]{2,1,0:T(1,128)} %reshape.520), calls=%async_computation.2 | async-start | bytes 1081344 | tf_op jit(solution)/shard_map/all_to_all | solution.py:170
  209.0 3.0 %copy-start.6 = (f32[4,128,132]{1,2,0:T(8,128)S(1)}, f32[4,128,132]{1,2,0:T(8,128)}, u32[]{:S(2)}) copy-start(f32[4,128,132]{1,2,0:T(8,128)} %multiply_add_fusion) | copy-start | bytes 811012
where the time goes:
time: 248 us; the launch traced here: 247 us
  local copies, waits for them, and re-layouts  77.7 us (31%)
  matrix products  49.3 us (20%)
  waiting for transfers between devices  38.6 us (16%)
  other arithmetic  36.6 us (15%)
  blocking collectives  27.7 us (11%)
  starting transfers between devices  14.4 us (6%)
    all_to_all x1, blocking collectives, local(): lax.all_to_all(solved, 'row', split_axis=2, concat_axis=3, tiled=True)  27.7 us
    dot_general x32, matrix products, one_radius(): jnp.einsum('qcpjt,cpjk->qtk', radius_block, synthesis, preferred_element_...  25.6 us
    another operation x65, other arithmetic  22.9 us
    unnamed x38, local copies, waits for them, and re-layouts  21.4 us
    dynamic_update_slice x32, local copies, waits for them, and re-layouts, local(): computed = lax.map(one_radius, latitudes)  20.8 us
    dot_general x32, matrix products, one_radius(): jnp.einsum('ftk,cpjk->fcpjt', products, analysis_fourier, preferred_eleme...  16 us
    all_to_all x1, waiting for transfers between devices, local(): lax.all_to_all(computed, 'ma', split_axis=3, concat_axis=5, tiled=True)  13.5 us
    all_to_all x1, waiting for transfers between devices, local(): lax.all_to_all(right_side.reshape(4, 2, radius_count, columns), 'row', sp...  12.7 us
  transfers between devices with their start and end apart: 3, of which 3 were waited for; matrix products, arithmetic and copies ran while one was open for 4% of the time, Pallas kernels for 0%

commit v1 on v0

--- a/solution.py
+++ b/solution.py
@@ -9,6 +9,28 @@
 SLOTS = 528
 ROTATION = 2.0
 SHELL_RADIUS = 16.0
+
+
+def cut_along(x, dim, size):
+    before, after = (x.shape[:dim], x.shape[dim + 1 :])
+    return jnp.moveaxis(x.reshape(*before, size, -1, *after), dim, 0)
+
+
+def joined_along(blocks, dim):
+    shape = list(blocks.shape[1:])
+    shape[dim] *= blocks.shape[0]
+    return jnp.moveaxis(blocks, 0, dim).reshape(shape)
+
+
+def pairwise_exchange(x, axis, split_dim, concat_dim):
+    count, here = (lax.axis_size(axis), lax.axis_index(axis))
+    tiles = cut_along(x, split_dim, count)
+    done = [tiles[here]]
+    for step in range(1, count):
+        sent = tiles[here ^ step]
+        done.append(lax.ppermute(sent, axis, [(i, i ^ step) for i in range(count)]))
+    tiles = jnp.stack(done)[here ^ jnp.arange(count)]
+    return joined_along(tiles, concat_dim)
 
 
 def slot_layout(pair_values):
@@ -179,7 +201,7 @@
         degree.reshape(columns), lax.axis_index("row") * share_size, share_size
     )
     solved = radial_solve(pencils, degree_share, diffusivity)
-    shells = lax.all_to_all(solved, "row", split_axis=2, concat_axis=3, tiled=True)
+    shells = pairwise_exchange(solved, "row", 2, 3)
     return shells * alive.reshape(columns)
 
 

time: 248 us -> 244 us (0.984)
  blocking collectives: 27.7 us -> 0 us
  waiting for transfers between devices: 38.6 us -> 56.2 us
  starting transfers between devices: 14.4 us -> 18.8 us
    all_to_all x1 -> x0, blocking collectives: 27.7 us -> none  [local(): lax.all_to_all(solved, 'row', split_axis=2, concat_axis=3, tiled=True)]
    ppermute x0 -> x3, waiting for transfers between devices: none -> 17.1 us  [pairwise_exchange(): done.append(lax.ppermute(sent, axis, [(i, i ^ step) for i in range(count)]))]
    ppermute x0 -> x3, starting transfers between devices: none -> 4.44 us  [pairwise_exchange(): done.append(lax.ppermute(sent, axis, [(i, i ^ step) for i in range(count)]))]
    another operation x65 -> x66, other arithmetic: 22.9 us -> 22.9 us
  transfers between devices with their start and end apart: 3 -> 6, of which waited for: 3 -> 5; matrix products, arithmetic and copies ran while one was open for 4% -> 4% of each run, Pallas kernels for 0% -> 0%
where the time goes in v1:
time: 244 us; the launch traced here: 241 us
  local copies, waits for them, and re-layouts  77.6 us (32%)
  waiting for transfers between devices  56.2 us (23%)
  matrix products  49.3 us (20%)
  other arithmetic  36.3 us (15%)
  starting transfers between devices  18.8 us (8%)
    dot_general x32, matrix products, one_radius(): jnp.einsum('qcpjt,cpjk->qtk', radius_block, synthesis, preferred_element_...  25.6 us
    another operation x65, other arithmetic  22.9 us
    unnamed x38, local copies, waits for them, and re-layouts  21.4 us
    dynamic_update_slice x32, local copies, waits for them, and re-layouts, local(): computed = lax.map(one_radius, latitudes)  20.8 us
    ppermute x3, waiting for transfers between devices, pairwise_exchange(): done.append(lax.ppermute(sent, axis, [(i, i ^ step) for i in range(count)]))  17.1 us
    dot_general x32, matrix products, one_radius(): jnp.einsum('ftk,cpjk->fcpjt', products, analysis_fourier, preferred_eleme...  16 us
    all_to_all x1, waiting for transfers between devices, local(): lax.all_to_all(computed, 'ma', split_axis=3, concat_axis=5, tiled=True)  13.5 us
    all_to_all x1, waiting for transfers between devices, local(): lax.all_to_all(right_side.reshape(4, 2, radius_count, columns), 'row', sp...  12.9 us
  transfers between devices with their start and end apart: 6, of which 5 were waited for; matrix products, arithmetic and copies ran while one was open for 4% of the time, Pallas kernels for 0%

profile of v1, /device:TPU:2, one launch (start us, length us, event | category | flops | bytes accessed | tf_op | source)
XLA Modules:
  0.0 240.7 jit_solution(2914263242028515154)
XLA Ops:
  0.0 1.3 dynamic_slice.16
  3.1 1.2 fusion.99
  5.2 1.0 copy-done.16
  7.4 11.3 %copy.33 = bf16[32,8,2,1,2,768]{0,4,2,1,3,5:T(2,128)(2,1)} copy(bf16[32,8,2,1,2,768]{5,0,4,2,1,3:T(8,128)(2,1)S(1)} %bitcast.179) | data formatting | bytes 3145728 | tf_op jit(solution)/shard_map/convert_element_type | solution.py:163
  18.6 9.5 %reshape.557 = bf16[8,2,49152]{2,1,0:T(2,128)(2,1)} reshape(bf16[768,1,8,2,2,32]{5,4,3,2,1,0:T(2,128)(2,1)} %bitcast.175) | data formatting | bytes 3145728
  28.2 4.4 %all-to-all-start = ((bf16[8,2,49152]{2,1,0:T(2,128)(2,1)}), bf16[8,2,49152]{2,1,0:T(2,128)(2,1)S(1)}, u32[]{:S(2)}, u32[]{:S(2)}) async-start(bf16[8,2,49152]{2,1,0:T(2,128)(2,1)} %reshape.557), calls=%async_computation | async-start | bytes 3145728 | tf_op jit(solution)/shard_map/all_to_all | solution.py:176
  33.2 1.2 fusion.68
  34.4 1.2 fusion.77
  39.4 12.7 %all-to-all-done = bf16[8,2,49152]{2,1,0:T(2,128)(2,1)S(1)} async-done(((bf16[8,2,49152]{2,1,0:T(2,128)(2,1)}), bf16[8,2,49152]{2,1,0:T(2,128)(2,1)S(1)}, u32[]{:S(2)}, u32[]{:S(2)}) %all-to-all-start) | async-done | bytes 1572896 | tf_op jit(solution)/shard_map/all_to_all | solution.py:176
  52.1 5.4 %reshape.558 = bf16[768,1,8,2,2,32]{5,4,3,2,1,0:T(2,128)(2,1)} reshape(bf16[8,2,49152]{2,1,0:T(2,128)(2,1)S(1)} %all-to-all-done) | data formatting | bytes 3145728
  57.5 11.0 %copy.34 = bf16[32,8,2,1,2,8,96]{6,5,4,1,2,0,3:T(8,128)(2,1)S(1)} copy(bf16[32,8,2,1,2,8,96]{0,4,2,1,6,5,3:T(2,128)(2,1)} %bitcast.176) | data formatting | bytes 3145728 | tf_op jit(solution)/shard_map/all_to_all | solution.py:176
  68.5 86.1 %while.10 = (s32[]{:T(128)}, bf16[32,4,2,8,2,96]{5,4,2,1,0,3:T(2,128)(2,1)}, bf16[32,8,2,8,2,96]{5,3,4,1,2,0:T(8,128)(2,1)S(1)}, bf16[2,8,2,1536]{3,1,2,0:T(8,12...) while((s32[]{:T(128)}, bf16[32,4,2,8,2,96]{5,4,2,1,0,3:T(2,128)(2,1)}, ...), condition=%wide.region_1.2_spmd, body=%wide.region_0.1_spmd.sunk | while | flops 122105856 | bytes 15680073 | solution.py:177
  154.6 5.1 %all-to-all-start.1 = ((bf16[32,4,2,8,2,96]{5,4,2,1,0,3:T(2,128)(2,1)}), bf16[32,4,2,8,2,96]{5,4,2,1,0,3:T(2,128)(2,1)S(1)}, u32[]{:S(2)}, u32[]{:S(2)}) async-start(bf16[32,4,2,8,2,96]{5,4,2,1,0,3:T(2,128)(2,1)} %get-tuple-element.32), calls=%async_computation.1 | async-start | bytes 2097152 | tf_op jit(solution)/shard_map/all_to_all | solution.py:178
  160.1 13.5 %all-to-all-done.1 = bf16[32,4,2,8,2,96]{5,4,2,1,0,3:T(2,128)(2,1)S(1)} async-done(((bf16[32,4,2,8,2,96]{5,4,2,1,0,3:T(2,128)(2,1)}), bf16[32,4,2,8,2,96]{5,4,2,1,0,3:T(2,128)(2,1)S(1)}, u32[]{:S(2)}, u32[]{:S(2)}) %all-to-all-start.1) | async-done | bytes 786464 | tf_op jit(solution)/shard_map/all_to_all | solution.py:178
  174.3 0.9 reshape.538
  175.2 2.1 fusion.13
  177.3 1.0 fusion.22
  178.3 2.9 %copy.41 = f32[4,2,32,528]{2,1,0,3:T(2,128)S(1)} copy(f32[4,2,32,528]{3,2,1,0:T(8,128)} %fusion.22) | data formatting | bytes 1081344 | tf_op jit(solution)/shard_map/mul | solution.py:191
  181.3 2.9 %reshape.559 = f32[4,1,33792]{2,1,0:T(1,128)} reshape(f32[528,4,2,32]{3,2,1,0:T(2,128)S(1)} %bitcast.177) | data formatting | bytes 1081344
  184.2 4.9 %all-to-all-start.2 = ((f32[4,1,33792]{2,1,0:T(1,128)}), f32[4,1,33792]{2,1,0:T(1,128)S(1)}, u32[]{:S(2)}, u32[]{:S(2)}) async-start(f32[4,1,33792]{2,1,0:T(1,128)} %reshape.559), calls=%async_computation.2 | async-start | bytes 1081344 | tf_op jit(solution)/shard_map/all_to_all | solution.py:192
  189.0 1.3 fusion.87
  191.2 12.9 %all-to-all-done.2 = f32[4,1,33792]{2,1,0:T(1,128)S(1)} async-done(((f32[4,1,33792]{2,1,0:T(1,128)}), f32[4,1,33792]{2,1,0:T(1,128)S(1)}, u32[]{:S(2)}, u32[]{:S(2)}) %all-to-all-start.2) | async-done | bytes 540704 | tf_op jit(solution)/shard_map/all_to_all | solution.py:192
  204.6 2.2 reduce.1
  206.8 1.9 reshape.560
  208.8 3.0 %copy.42 = f32[4,2,32,4,132]{4,2,3,1,0:T(8,128)} copy(f32[4,2,32,4,132]{2,1,0,4,3:T(2,128)S(1)} %bitcast.178) | data formatting | bytes 1081344 | tf_op jit(solution)/shard_map/all_to_all | solution.py:192
  211.7 3.2 %fusion.15 = f32[4,2,128,132]{2,3,1,0:T(8,128)S(1)} fusion(f32[4,2,128,132]{3,2,1,0:T(8,128)} %bitcast.184, f32[4,128,132]{1,2,0:T(8,128)S(1)} %copy-done.6, s32[128]{0:T(128)S(1)} %iota_add_fusion.1), kind=kOutput, calls=%fused_computation.33 | convolution fusion | flops 207917056 | bytes 1352192 | tf_op jit(solution)/shard_map/jk,fcks->fcjs/dot_general | solution.py:125
  214.9 0.9 convolution_bitcast_fusion.3
  216.3 2.0 collective-permute-start.1
  218.4 2.4 collective-permute-start.2
  220.7 7.5 %collective-permute-done = f32[4,2,32,132]{3,2,1,0:T(8,128)S(1)} collective-permute-done((f32[4,2,32,132]{3,2,1,0:T(8,128)S(1)}, f32[4,2,32,132]{3,2,1,0:T(8,128)S(1)}, u32[]{:S(2)}, u32[]{:S(2)}) %collective-permute-start) | collective-permute-done | bytes 135200 | tf_op jit(solution)/shard_map/ppermute | solution.py:31
  228.2 9.6 %collective-permute-done.1 = f32[4,2,32,132]{3,2,1,0:T(8,128)S(1)} collective-permute-done((f32[4,2,32,132]{3,2,1,0:T(8,128)S(1)}, f32[4,2,32,132]{3,2,1,0:T(8,128)S(1)}, u32[]{:S(2)}, u32[]{:S(2)}) %collective-permute-start.1) | collective-permute-done | bytes 135200 | tf_op jit(solution)/shard_map/ppermute | solution.py:31
  239.8 0.9 broadcast_multiply_fusion
  (234 shorter events, 97.2 us)
Async XLA Ops:
  0.0 4.3 %copy-start = (bf16[528,768]{1,0:T(8,128)(2,1)S(1)}, bf16[528,768]{1,0:T(8,128)(2,1)}, u32[]{:S(2)}) copy-start(bf16[528,768]{1,0:T(8,128)(2,1)} %param.10) | copy-start | bytes 2433028
  1.9 0.5 copy-start.10
  4.2 33.7 %copy-start.1 = (f32[4,2,32,528]{3,2,1,0:T(8,128)}, f32[4,2,32,528]{3,2,1,0:T(8,128)S(1)}, u32[]{:S(2)}) copy-start(f32[4,2,32,528]{3,2,1,0:T(8,128)S(1)} %get-tuple-element.47) | copy-start | bytes 1622020
  5.1 1.1 copy-start.16
  28.2 4.4 %copy-start.12 = (s32[8]{0:T(128)S(1)}, s32[8]{0:T(128)}, u32[]{:S(2)}) copy-start(s32[8]{0:T(128)} %param.12) | copy-start | bytes 100
  28.2 23.9 %all-to-all-start = ((bf16[8,2,49152]{2,1,0:T(2,128)(2,1)}), bf16[8,2,49152]{2,1,0:T(2,128)(2,1)S(1)}, u32[]{:S(2)}, u32[]{:S(2)}) async-start(bf16[8,2,49152]{2,1,0:T(2,128)(2,1)} %reshape.557), calls=%async_computation | async-start | bytes 3145728 | tf_op jit(solution)/shard_map/all_to_all | solution.py:176
  57.5 11.0 %copy-start.7 = (bf16[2,8,2,1536]{3,1,2,0:T(8,128)(2,1)S(1)}, bf16[2,8,2,1536]{3,1,2,0:T(8,128)(2,1)}, u32[]{:S(2)}) copy-start(bf16[2,8,2,1536]{3,1,2,0:T(8,128)(2,1)} %fusion.27) | copy-start | bytes 294916
  154.6 5.1 %copy-start.3 = (f32[1,2,32,1,528]{4,2,1,3,0:T(8,128)S(1)}, f32[1,2,32,1,528]{4,2,1,3,0:T(8,128)}, u32[]{:S(2)}) copy-start(f32[1,2,32,1,528]{4,2,1,3,0:T(8,128)} %get-tuple-element.58) | copy-start | bytes 405508
  154.6 5.3 %copy-start.4 = (f32[1,32,1,528]{3,1,0,2:T(8,128)S(1)}, f32[1,32,1,528]{3,1,0,2:T(8,128)}, u32[]{:S(2)}) copy-start(f32[1,32,1,528]{3,1,0,2:T(8,128)} %get-tuple-element.65) | copy-start | bytes 202756
  154.6 5.3 %copy-start.5 = (f32[1,32,1,528]{3,1,2,0:T(8,128)S(1)}, f32[1,32,1,528]{3,1,2,0:T(8,128)}, u32[]{:S(2)}) copy-start(f32[1,32,1,528]{3,1,2,0:T(8,128)} %get-tuple-element.80) | copy-start | bytes 202756
  154.6 5.3 %copy-start.8 = (f32[528]{0:T(1024)S(1)}, f32[528]{0:T(1024)}, u32[]{:S(2)}) copy-start(f32[528]{0:T(1024)} %get-tuple-element.79) | copy-start | bytes 6340
  154.6 5.3 %copy-start.9 = (f32[528]{0:T(1024)S(1)}, f32[528]{0:T(1024)}, u32[]{:S(2)}) copy-start(f32[528]{0:T(1024)} %fusion.77) | copy-start | bytes 6340
  154.6 19.0 %all-to-all-start.1 = ((bf16[32,4,2,8,2,96]{5,4,2,1,0,3:T(2,128)(2,1)}), bf16[32,4,2,8,2,96]{5,4,2,1,0,3:T(2,128)(2,1)S(1)}, u32[]{:S(2)}, u32[]{:S(2)}) async-start(bf16[32,4,2,8,2,96]{5,4,2,1,0,3:T(2,128)(2,1)} %get-tuple-element.32), calls=%async_computation.1 | async-start | bytes 2097152 | tf_op jit(solution)/shard_map/all_to_all | solution.py:178
  173.6 1.6 copy-start.11
  175.2 2.1 copy-start.2
  175.2 2.1 copy-start.15
  181.2 9.1 %copy-start.14 = (f32[128]{0:T(128)S(1)}, f32[128]{0:T(128)}, u32[]{:S(2)}) copy-start(f32[128]{0:T(128)} %multiply_multiply_fusion.2) | copy-start | bytes 1540
  181.2 9.2 %copy-start.13 = (f32[4]{0:T(128)S(1)}, f32[4]{0:T(128)}, u32[]{:S(2)}) copy-start(f32[4]{0:T(128)} %param.13) | copy-start | bytes 52
  184.2 19.9 %all-to-all-start.2 = ((f32[4,1,33792]{2,1,0:T(1,128)}), f32[4,1,33792]{2,1,0:T(1,128)S(1)}, u32[]{:S(2)}, u32[]{:S(2)}) async-start(f32[4,1,33792]{2,1,0:T(1,128)} %reshape.559), calls=%async_computation.2 | async-start | bytes 1081344 | tf_op jit(solution)/shard_map/all_to_all | solution.py:192
  208.7 3.0 %copy-start.6 = (f32[4,128,132]{1,2,0:T(8,128)S(1)}, f32[4,128,132]{1,2,0:T(8,128)}, u32[]{:S(2)}) copy-start(f32[4,128,132]{1,2,0:T(8,128)} %multiply_add_fusion) | copy-start | bytes 811012
  216.3 11.9 %collective-permute-start = (f32[4,2,32,132]{3,2,1,0:T(8,128)S(1)}, f32[4,2,32,132]{3,2,1,0:T(8,128)S(1)}, u32[]{:S(2)}, u32[]{:S(2)}) collective-permute-start(f32[4,2,32,132]{3,2,1,0:T(8,128)S(1)} %get-tuple-element.54), channel_id=1, source_target_pairs={{0,8},{8,0},{16,24},{24,16},{1,9},{9,1},{17,25},{25,17},{2,10},{10... | collective-permute-start | bytes 405512 | tf_op jit(solution)/shard_map/ppermute | solution.py:31
  216.3 21.4 %collective-permute-start.1 = (f32[4,2,32,132]{3,2,1,0:T(8,128)S(1)}, f32[4,2,32,132]{3,2,1,0:T(8,128)S(1)}, u32[]{:S(2)}, u32[]{:S(2)}) collective-permute-start(f32[4,2,32,132]{3,2,1,0:T(8,128)S(1)} %get-tuple-element.53), channel_id=1, source_target_pairs={{0,16},{8,24},{16,0},{24,8},{1,17},{9,25},{17,1},{25,9},{2,18},{10... | collective-permute-start | bytes 405512 | tf_op jit(solution)/shard_map/ppermute | solution.py:31
  218.4 19.4 %collective-permute-start.2 = (f32[4,2,32,132]{3,2,1,0:T(8,128)S(1)}, f32[4,2,32,132]{3,2,1,0:T(8,128)S(1)}, u32[]{:S(2)}, u32[]{:S(2)}) collective-permute-start(f32[4,2,32,132]{3,2,1,0:T(8,128)S(1)} %get-tuple-element.52), channel_id=1, source_target_pairs={{0,24},{8,16},{16,8},{24,0},{1,25},{9,17},{17,9},{25,1},{2,26},{10... | collective-permute-start | bytes 405512 | tf_op jit(solution)/shard_map/ppermute | solution.py:31
